TPU v7x, 32 devices: a whole 2x2x4 slice. The times are simulated.
32 devices in a mesh: slide: 2 (over y), seq: 8 (over z, x), head: 2 (over core).
Axes of the slice: x: 2, y: 2, z: 4, core: 2. Of those that a mesh axis runs over, the one named last changes fastest.
Arguments:
- tokens: bfloat16 [8192, 768], P(('slide', 'seq')), parts along dimension 0
- tile_index: int32 [8192], P(('slide', 'seq')), parts along dimension 0, may hold values from 0 to 8191, as said below
- dilation_offset: int32 [2, 16], P(None, 'head'), may hold values from 0 to 3, as said below
- norm_gain: float32 [768], replicated
- w_query: bfloat16 [768, 768], P(None, 'head'), may hold values from -0.21875 to 0.21875
- w_key: bfloat16 [768, 768], P(None, 'head'), may hold values from -0.21875 to 0.21875
- w_value: bfloat16 [768, 768], P(None, 'head'), may hold values from -0.21875 to 0.21875
- w_out: bfloat16 [768, 768], P('head'), may hold values from -0.21875 to 0.21875
Outputs:
- mixed: float32 [8192, 768], P(('slide', 'seq'), 'head'), parts along dimension 0
There are 2 independent parts, one for each index of `slide`. A program takes and returns all parts, laid end to end along the dimension named above; an argument that names none is the same for every part. Nothing has to cross between parts.
Inputs may be any that keep to these rules, and one draw needn't show every extreme that they name: `tile_index`: strictly rising along a slide; tile p holds 2 p or 2 p + 1, the first holds 0 and the last 8191. `dilation_offset`: row 0 is below 2 and holds 1 at some head; row 1 is below 4 and holds 3 at some head (2 and 4 follow the number of devices along seq as the steps state).
All inputs are finite; a program needn't handle non-finite values.
Results may differ from a plain program's by a relative error of at most 0.0074.
Values may be sent and summed in bfloat16 or wider, within the bound.
A program may use at most 64 MiB of HBM per device.

v0:
```python
import jax
import jax.numpy as jnp
from jax import lax
from jax.sharding import PartitionSpec as P

D = 768
HEAD_DIM = 48
GRID_W = 256


def partner(value, axis, stride):
    return lax.ppermute(value, axis, [(i, i ^ 1 << stride) for i in range(lax.axis_size(axis))])


def position_table(tile_index):
    quarter = D // 4
    freq = jnp.exp(-jnp.log(10000.0) * jnp.arange(quarter, dtype=jnp.float32) / quarter)
    row_pos = (tile_index // GRID_W).astype(jnp.float32)[:, None] * freq[None, :]
    col_pos = (tile_index % GRID_W).astype(jnp.float32)[:, None] * freq[None, :]
    return jnp.concatenate(
        [jnp.sin(row_pos), jnp.cos(row_pos), jnp.sin(col_pos), jnp.cos(col_pos)], axis=1
    )


def normalize(hidden, gain):
    mean = jnp.mean(hidden, axis=1, keepdims=True)
    centred = hidden - mean
    spread = jnp.mean(centred * centred, axis=1, keepdims=True)
    return (centred * lax.rsqrt(spread + 1e-05) * gain[None, :]).astype(jnp.bfloat16)


def attend(query_rows, key_rows, value_rows):
    score_scale = HEAD_DIM ** (-0.5)
    logit_scores = (
        lax.dot_general(
            query_rows, key_rows, (((1,), (1,)), ((), ())), preferred_element_type=jnp.float32
        )
        * score_scale
    )
    top = jnp.max(logit_scores, axis=1, keepdims=True)
    weights = jnp.exp(logit_scores - top)
    total_length = jnp.sum(weights, axis=1, keepdims=True)
    mixed = (
        jnp.dot(weights.astype(jnp.bfloat16), value_rows, preferred_element_type=jnp.float32)
        / total_length
    )
    return (mixed, top[:, 0] + jnp.log(total_length[:, 0]))


def attend_heads(query_rows, key_rows, value_rows):
    return lax.map(
        lambda trio: attend(trio[0], trio[1], trio[2]), (query_rows, key_rows, value_rows)
    )


def head_major(flat):
    return flat.reshape(flat.shape[0], -1, HEAD_DIM).transpose(1, 0, 2)


def row_major(split):
    return split.transpose(1, 0, 2).reshape(split.shape[1], -1)


def select_rows(split, picks):
    local_heads, count, width = split.shape
    rate = picks.shape[1]
    grouped = split.reshape(local_heads, count // rate, rate, width)
    return jnp.sum(jnp.where(picks[:, None, :, None], grouped, jnp.zeros((), split.dtype)), axis=2)


def spread_rows(mixed, lse, picks):
    local_heads, count, width = mixed.shape
    rate = picks.shape[1]
    full = jnp.where(picks[:, None, :, None], mixed[:, :, None, :], 0.0).reshape(
        local_heads, count * rate, width
    )
    lse_full = jnp.where(picks[:, None, :], lse[:, :, None], 0.0).reshape(local_heads, count * rate)
    taken_mask = jnp.broadcast_to(picks[:, None, :], (local_heads, count, rate)).reshape(
        local_heads, count * rate
    )
    return (full, lse_full, taken_mask)


def combine(out_one, lse_one, out_two, lse_two, mask_two, out_three, lse_three, mask_three):
    top = jnp.maximum(lse_one, jnp.where(mask_two, lse_two, lse_one))
    top = jnp.maximum(top, jnp.where(mask_three, lse_three, lse_one))
    weight_one = jnp.exp(lse_one - top)
    weight_two = jnp.where(mask_two, jnp.exp(lse_two - top), 0.0)
    weight_three = jnp.where(mask_three, jnp.exp(lse_three - top), 0.0)
    summed = (
        weight_one[..., None] * out_one
        + weight_two[..., None] * out_two
        + weight_three[..., None] * out_three
    )
    return summed / (weight_one + weight_two + weight_three)[..., None]


def body(tokens, tile_index, dilation_offset, norm_gain, w_query, w_key, w_value, w_out):
    seq_devs = lax.axis_size("seq")
    rate_two = min(16, seq_devs // 4)
    rate_three = seq_devs // 2
    group_devs = 2 * rate_two
    hidden = tokens.astype(jnp.float32) + position_table(tile_index)
    normed = normalize(hidden, norm_gain)
    query_rows = jnp.dot(normed, w_query, preferred_element_type=jnp.float32).astype(jnp.bfloat16)
    key_rows = jnp.dot(normed, w_key, preferred_element_type=jnp.float32).astype(jnp.bfloat16)
    value_rows = jnp.dot(normed, w_value, preferred_element_type=jnp.float32).astype(jnp.bfloat16)
    q_split = head_major(query_rows)
    k_split = head_major(key_rows)
    v_split = head_major(value_rows)
    picks_two = dilation_offset[0][:, None] == jnp.arange(rate_two, dtype=jnp.int32)[None, :]
    picks_three = dilation_offset[1][:, None] == jnp.arange(rate_three, dtype=jnp.int32)[None, :]
    keys_two = row_major(select_rows(k_split, picks_two))
    values_two = row_major(select_rows(v_split, picks_two))
    keys_three = row_major(select_rows(k_split, picks_three))
    values_three = row_major(select_rows(v_split, picks_three))
    partner_keys, partner_values = partner((key_rows, value_rows), "seq", 0)
    group_keys, group_values = (keys_two, values_two)
    for bit in range(group_devs.bit_length() - 1):
        other_keys, other_values = partner((group_keys, group_values), "seq", bit)
        group_keys = jnp.concatenate([group_keys, other_keys], axis=0)
        group_values = jnp.concatenate([group_values, other_values], axis=0)
    wide_keys, wide_values = (
        lax.all_gather(keys_three, "seq", axis=0, tiled=True),
        lax.all_gather(values_three, "seq", axis=0, tiled=True),
    )
    dense_keys = head_major(jnp.concatenate([key_rows, partner_keys], axis=0))
    dense_values = head_major(jnp.concatenate([value_rows, partner_values], axis=0))
    out_one, lse_one = attend_heads(q_split, dense_keys, dense_values)
    mixed_two, lse_two_rows = attend_heads(
        select_rows(q_split, picks_two), head_major(group_keys), head_major(group_values)
    )
    out_two, lse_two, mask_two = spread_rows(mixed_two, lse_two_rows, picks_two)
    mixed_three, lse_three_rows = attend_heads(
        select_rows(q_split, picks_three), head_major(wide_keys), head_major(wide_values)
    )
    out_three, lse_three, mask_three = spread_rows(mixed_three, lse_three_rows, picks_three)
    attended = combine(
        out_one, lse_one, out_two, lse_two, mask_two, out_three, lse_three, mask_three
    )
    attn = row_major(attended).astype(jnp.bfloat16)
    local_width = D // lax.axis_size("head")
    residual = lax.dynamic_slice_in_dim(
        hidden, lax.axis_index("head") * local_width, local_width, 1
    )
    partial_value = jnp.dot(attn, w_out, preferred_element_type=jnp.float32)
    projected = lax.psum_scatter(partial_value, "head", scatter_dimension=1, tiled=True)
    return residual + projected


def solution(mesh):
    placed = (
        P(("slide", "seq"), None),
        P(("slide", "seq")),
        P(None, "head"),
        P(),
        P(None, "head"),
        P(None, "head"),
        P(None, "head"),
        P("head", None),
    )
    return jax.shard_map(
        body, mesh=mesh, in_specs=placed, out_specs=P(("slide", "seq"), "head"), check_vma=False
    )
```

profile of v0, /device:TPU:0, one launch (start us, length us, event | category | flops | bytes accessed | tf_op | source)
XLA Modules:
  0.0 232.7 jit_solution(9864820358420318905)
XLA Ops:
  7.4 3.7 %multiply_sine_fusion.1 = (f32[512,192]{1,0:T(8,128)S(1)}, f32[512,192]{1,0:T(8,128)S(1)}, f32[512,192]{1,0:T(8,128)S(1)}, f32[512,192]{1,0:T(8,128)S(1)}) fusion(f32[192]{0:T(256)S(1)} %multiply_exponential_fusion, f32[512]{0:T(512)S(1)} %get-tuple-element.222, f32[512]{0:T(512)S(1)} %get-tuple-element.223), kind=kLoop, calls=%fused_computation.82 | loop fusion | flops 196608 | bytes 1577728 | tf_op jit(solution)/shard_map/sin | solution.py:21
  14.4 2.9 %collective-permute-start.1 = (bf16[512,384]{0,1:T(8,128)(2,1)}, bf16[512,384]{0,1:T(8,128)(2,1)}, u32[]{:S(2)}, u32[]{:S(2)}) collective-permute-start(bf16[512,384]{0,1:T(8,128)(2,1)} %convolution_convert_fusion), channel_id=1, source_target_pairs={{0,2},{2,0},{4,6},{6,4},{8,10},{10,8},{12,14},{14,12},{1,3},{3,1},... | collective-permute-start | bytes 1179656 | tf_op jit(solution)/shard_map/ppermute | solution.py:12
  25.8 3.5 %select_reduce_fusion.3 = (bf16[8,256,48]{2,0,1:T(8,128)(2,1)}, bf16[8,256,48]{2,0,1:T(8,128)(2,1)}, bf16[8,256,48]{2,0,1:T(8,128)(2,1)S(1)}) fusion(pred[8,2]{0,1:T(4,128)(4,1)S(1)} %iota_compare_fusion.1, bf16[512,8,48]{2,1,0:T(8,128)(2,1)S(1)} %copy.70, bf16[512,8,48]{2,1,0:T(8,128)(2,1)S(1)} %copy.67, bf16[8,512,48]{2,0,1:T(8,128)(2,1)} %copy.66), kind=kLoop, calls=%fused_computation.71 | loop fusion | flops 884736 | bytes 1769488 | tf_op jit(solution)/shard_map/reduce_sum | solution.py:68
  29.3 2.0 copy.72
  31.3 2.0 collective-permute-start.4
  34.8 3.5 %select_reduce_fusion = (bf16[8,128,48]{2,0,1:T(8,128)(2,1)}, bf16[8,128,48]{2,0,1:T(8,128)(2,1)}, bf16[8,128,48]{2,0,1:T(8,128)(2,1)}) fusion(pred[8,4]{0,1:T(4,128)(4,1)S(1)} %iota_compare_fusion, bf16[512,8,48]{2,1,0:T(8,128)(2,1)S(1)} %copy.70, bf16[512,8,48]{2,1,0:T(8,128)(2,1)S(1)} %copy.67, bf16[8,512,48]{2,0,1:T(8,128)(2,1)} %copy.66), kind=kLoop, calls=%fused_computation.68 | loop fusion | flops 1032192 | bytes 1474592 | tf_op jit(solution)/shard_map/reduce_sum | solution.py:68
  39.5 30.2 %all_gather.6 = bf16[1024,384]{0,1:T(8,128)(2,1)S(1)} all-gather(bf16[128,384]{0,1:T(8,128)(2,1)S(1)} %bitcast.200), channel_id=1, replica_groups=mesh['slide'=2,'seq'=8,'head'=2] {'seq'}, dimensions={0}, use_global_device_ids=true | all-gather | bytes 884736 | tf_op jit(solution)/shard_map/all_gather | solution.py:124
  70.8 28.3 %all_gather.7 = bf16[1024,384]{0,1:T(8,128)(2,1)S(1)} all-gather(bf16[128,384]{0,1:T(8,128)(2,1)S(1)} %bitcast.201), channel_id=1, replica_groups=mesh['slide'=2,'seq'=8,'head'=2] {'seq'}, dimensions={0}, use_global_device_ids=true | all-gather | bytes 884736 | tf_op jit(solution)/shard_map/all_gather | solution.py:125
  99.9 17.8 %while.38 = (s32[]{:T(128)}, f32[8,128,48]{1,2,0:T(8,128)}, f32[8,128]{1,0:T(8,128)S(1)}, bf16[8,128,48]{2,1,0:T(8,128)(2,1)}, bf16[8,1024,48]{1,2,0:T(8,128)(2,...) while((s32[]{:T(128)}, f32[8,128,48]{1,2,0:T(8,128)}, f32[8,128]{1,0:T(8,128)S(1)}, ...), condition=%wide.region_19.20_spmd, body=%wide.region_16.19_spmd.sunk | while | flops 25958272 | bytes 1834073 | solution.py:51
  119.3 2.3 %copy.61 = bf16[512,8,48]{2,0,1:T(8,128)(2,1)} copy(bf16[512,8,48]{0,2,1:T(8,128)(2,1)} %bitcast.193) | data formatting | bytes 786432 | tf_op jit(solution)/shard_map/reshape | solution.py:57
  133.8 34.3 %while.36 = (s32[]{:T(128)}, f32[8,512,48]{1,2,0:T(8,128)}, f32[8,512]{1,0:T(8,128)S(1)}, bf16[8,512,48]{2,1,0:T(8,128)(2,1)}, bf16[8,1024,48]{2,1,0:T(8,128)(2,...) while((s32[]{:T(128)}, f32[8,512,48]{1,2,0:T(8,128)}, f32[8,512]{1,0:T(8,128)S(1)}, ...), condition=%wide.region_5.6_spmd, body=%wide.region_2.5_spmd.sunk | while | flops 104881664 | bytes 7067737 | solution.py:51
  135.9 2.2 fusion.91
  140.2 2.2 fusion.91
  144.5 2.2 fusion.91
  148.8 2.2 fusion.91
  153.1 2.2 fusion.91
  157.4 2.2 fusion.91
  161.6 2.2 fusion.91
  165.9 2.2 fusion.91
  168.9 3.1 %copy.88 = f32[8,512,48]{2,0,1:T(8,128)} copy(f32[8,512,48]{1,2,0:T(8,128)} %get-tuple-element.107) | data formatting | bytes 1572864 | tf_op jit(solution)/shard_map/while | solution.py:51
  172.1 2.1 maximum_bitcast_fusion.1
  175.3 27.4 %while.37 = (s32[]{:T(128)}, f32[8,256,48]{1,2,0:T(8,128)}, f32[8,256]{1,0:T(8,128)S(1)}, bf16[8,256,48]{2,1,0:T(8,128)(2,1)}, bf16[8,1024,48]{1,2,0:T(8,128)(2,...) while((s32[]{:T(128)}, f32[8,256,48]{1,2,0:T(8,128)}, f32[8,256]{1,0:T(8,128)S(1)}, ...), condition=%wide.region_12.13_spmd, body=%wide.region_9.12_spmd.sunk | while | flops 51916544 | bytes 3469401 | solution.py:51
  180.3 1.9 fusion.96
  183.7 1.9 fusion.96
  187.2 1.9 fusion.96
  194.0 1.9 fusion.96
  197.4 1.9 fusion.96
  200.8 1.9 fusion.96
  203.5 2.5 %copy.89 = f32[8,256,48]{2,0,1:T(8,128)} copy(f32[8,256,48]{1,2,0:T(8,128)} %get-tuple-element.108) | data formatting | bytes 786432 | tf_op jit(solution)/shard_map/while | solution.py:51
  208.2 5.0 %fusion.50 = bf16[8,512,48]{2,0,1:T(8,128)(2,1)} fusion(f32[8,512,48]{2,0,1:T(8,128)S(1)} %copy-done.3, f32[8,512]{0,1:T(8,128)S(1)} %get-tuple-element.206, f32[8,128,48]{2,0,1:T(8,128)S(1)} %copy.90, f32[8,512]{0,1:T(8,128)S(1)} %get-tuple-element.209, f32[8,256,48]{2,0,1:T(8,128)S(1)} %copy-done.4, f32[8,512]{0,1:T(8,128)S(1)} %get-tuple-element.207, ...), kind=kLoop, calls=%fused_computation.61 | loop fusion | flops 1769472 | bytes 1843200 | tf_op jit(solution)/shard_map/convert_element_type | solution.py:141
  216.9 6.9 %reduce-scatter.2.cloned.1.call-done = f32[512,384]{1,0:T(8,128)} async-done(((f32[512,768]{1,0:T(8,128)}), f32[512,384]{1,0:T(8,128)}) %reduce-scatter.2.cloned.1.call-update) | async-done | bytes 786448 | tf_op jit(solution)/shard_map/reduce_scatter | solution.py:147
  223.8 2.1 dynamic-slice_add_fusion
  (194 shorter events, 90.0 us)
Async XLA Ops:
  6.5 208.6 %copy-start = (bf16[384,768]{1,0:T(8,128)(2,1)S(1)}, bf16[384,768]{1,0:T(8,128)(2,1)}, u32[]{:S(2)}) copy-start(bf16[384,768]{1,0:T(8,128)(2,1)} %param.21) | copy-start | bytes 1769476
  6.5 4.5 %copy-start.9 = (bf16[512,768]{1,0:T(8,128)(2,1)S(1)}, bf16[512,768]{1,0:T(8,128)(2,1)}, u32[]{:S(2)}) copy-start(bf16[512,768]{1,0:T(8,128)(2,1)} %param.14) | copy-start | bytes 2359300
  6.5 217.2 %reduce-scatter.2.cloned.1.call-start = ((), (), s32[]{:S(2)}) async-start(), calls=%async_computation.1 | async-start | bytes 2359296 | tf_op jit(solution)/shard_map/reduce_scatter | solution.py:147
  11.1 0.9 copy-start.11
  11.6 2.8 %copy-start.1 = (f32[512,768]{1,0:T(8,128)}, f32[512,768]{1,0:T(8,128)S(1)}, u32[]{:S(2)}) copy-start(f32[512,768]{1,0:T(8,128)S(1)} %get-tuple-element.211) | copy-start | bytes 4718596
  11.7 1.5 copy-start.13
  12.0 5.4 %copy-start.14 = (bf16[768,384]{1,0:T(8,128)(2,1)S(1)}, bf16[768,384]{1,0:T(8,128)(2,1)}, u32[]{:S(2)}) copy-start(bf16[768,384]{1,0:T(8,128)(2,1)} %param.19) | copy-start | bytes 1769476
  13.1 5.5 %copy-start.8 = (bf16[512,768]{1,0:T(8,128)(2,1)}, bf16[512,768]{1,0:T(8,128)(2,1)S(1)}, u32[]{:S(2)}) copy-start(bf16[512,768]{1,0:T(8,128)(2,1)S(1)} %multiply_convert_fusion) | copy-start | bytes 2359300
  14.4 113.4 %collective-permute-start.1 = (bf16[512,384]{0,1:T(8,128)(2,1)}, bf16[512,384]{0,1:T(8,128)(2,1)}, u32[]{:S(2)}, u32[]{:S(2)}) collective-permute-start(bf16[512,384]{0,1:T(8,128)(2,1)} %convolution_convert_fusion), channel_id=1, source_target_pairs={{0,2},{2,0},{4,6},{6,4},{8,10},{10,8},{12,14},{14,12},{1,3},{3,1},... | collective-permute-start | bytes 1179656 | tf_op jit(solution)/shard_map/ppermute | solution.py:12
  18.6 112.2 %collective-permute-start = (bf16[512,384]{0,1:T(8,128)(2,1)}, bf16[512,384]{0,1:T(8,128)(2,1)}, u32[]{:S(2)}, u32[]{:S(2)}) collective-permute-start(bf16[512,384]{0,1:T(8,128)(2,1)} %convolution_convert_fusion.1), channel_id=1, source_target_pairs={{0,2},{2,0},{4,6},{6,4},{8,10},{10,8},{12,14},{14,12},{1,3},{3,1},... | collective-permute-start | bytes 1179656 | tf_op jit(solution)/shard_map/ppermute | solution.py:12
  20.5 5.3 %copy-start.12 = (s32[2,8]{1,0:T(2,128)S(1)}, s32[2,8]{1,0:T(2,128)}, u32[]{:S(2)}) copy-start(s32[2,8]{1,0:T(2,128)} %param.16) | copy-start | bytes 196
  24.1 1.7 copy-start.5
  31.3 90.8 %collective-permute-start.4 = (bf16[256,384]{0,1:T(8,128)(2,1)}, bf16[256,384]{0,1:T(8,128)(2,1)}, u32[]{:S(2)}, u32[]{:S(2)}) collective-permute-start(bf16[256,384]{0,1:T(8,128)(2,1)} %bitcast.36), channel_id=1, source_target_pairs={{0,2},{2,0},{4,6},{6,4},{8,10},{10,8},{12,14},{14,12},{1,3},{3,1},... | collective-permute-start | bytes 589832 | tf_op jit(solution)/shard_map/ppermute | solution.py:12
  34.7 89.9 %collective-permute-start.2 = (bf16[256,384]{0,1:T(8,128)(2,1)S(1)}, bf16[256,384]{0,1:T(8,128)(2,1)}, u32[]{:S(2)}, u32[]{:S(2)}) collective-permute-start(bf16[256,384]{0,1:T(8,128)(2,1)S(1)} %bitcast.189), channel_id=1, source_target_pairs={{0,2},{2,0},{4,6},{6,4},{8,10},{10,8},{12,14},{14,12},{1,3},{3,1},... | collective-permute-start | bytes 589832 | tf_op jit(solution)/shard_map/ppermute | solution.py:12
  38.3 60.8 %copy-start.7 = (bf16[8,128,48]{2,0,1:T(8,128)(2,1)S(1)}, bf16[8,128,48]{2,0,1:T(8,128)(2,1)}, u32[]{:S(2)}) copy-start(bf16[8,128,48]{2,0,1:T(8,128)(2,1)} %get-tuple-element.169) | copy-start | bytes 294916
  117.7 4.2 %copy-start.10 = (f32[8,128,48]{1,2,0:T(8,128)S(1)}, f32[8,128,48]{1,2,0:T(8,128)}, u32[]{:S(2)}) copy-start(f32[8,128,48]{1,2,0:T(8,128)} %get-tuple-element.109) | copy-start | bytes 589828
  124.0 48.1 %collective-permute-start.5 = (bf16[512,384]{0,1:T(8,128)(2,1)}, bf16[512,384]{0,1:T(8,128)(2,1)}, u32[]{:S(2)}, u32[]{:S(2)}) collective-permute-start(bf16[512,384]{0,1:T(8,128)(2,1)} %pad_maximum_fusion.3), channel_id=1, source_target_pairs={{0,4},{2,6},{4,0},{6,2},{8,12},{10,14},{12,8},{14,10},{1,5},{3,7},... | collective-permute-start | bytes 1179656 | tf_op jit(solution)/shard_map/ppermute | solution.py:12
  126.3 47.9 %collective-permute-start.3 = (bf16[512,384]{0,1:T(8,128)(2,1)}, bf16[512,384]{0,1:T(8,128)(2,1)}, u32[]{:S(2)}, u32[]{:S(2)}) collective-permute-start(bf16[512,384]{0,1:T(8,128)(2,1)} %pad_maximum_fusion.2), channel_id=1, source_target_pairs={{0,4},{2,6},{4,0},{6,2},{8,12},{10,14},{12,8},{14,10},{1,5},{3,7},... | collective-permute-start | bytes 1179656 | tf_op jit(solution)/shard_map/ppermute | solution.py:12
  202.7 5.3 %copy-start.6 = (f32[8,512]{0,1:T(8,128)S(1)}, f32[8,512]{0,1:T(8,128)}, u32[]{:S(2)}) copy-start(f32[8,512]{0,1:T(8,128)} %copy.87) | copy-start | bytes 49156
  203.5 4.7 %copy-start.3 = (f32[8,512,48]{2,0,1:T(8,128)S(1)}, f32[8,512,48]{2,0,1:T(8,128)}, u32[]{:S(2)}) copy-start(f32[8,512,48]{2,0,1:T(8,128)} %copy.88) | copy-start | bytes 2359300
  206.0 2.3 copy-start.4
  215.1 8.7 %copy-start.2 = (f32[512,768]{1,0:T(8,128)S(1)}, f32[512,768]{1,0:T(8,128)}, u32[]{:S(2)}) copy-start(f32[512,768]{1,0:T(8,128)} %copy-done.1) | copy-start | bytes 4718596
Sparse Core Ops, SparseCore 0:
  217.0 6.6 reduce-scatter.1
where the time goes:
time: 235 us; the launch traced here: 233 us
  matrix products  75.7 us (32%)
  blocking collectives  58.5 us (25%)
  other arithmetic  37.8 us (16%)
  local copies, waits for them, and re-layouts  32.7 us (14%)
  between operations  13.7 us (6%)
  starting transfers between devices  7.07 us (3%)
  waiting for transfers between devices  6.89 us (3%)
    dot_general x24, matrix products, attend(): jnp.dot(weights.astype(jnp.bfloat16), value_rows, preferred_element_type=...  39.4 us
    all_gather x1, blocking collectives, body(): lax.all_gather(keys_three, 'seq', axis=0, tiled=True)  30.2 us
    dot_general x24, matrix products, attend(): lax.dot_general(query_rows, key_rows, (((1,), (1,)), ((), ())), preferred...  30.2 us
    all_gather x1, blocking collectives, body(): lax.all_gather(values_three, 'seq', axis=0, tiled=True)  28.3 us
    while x8, local copies, waits for them, and re-layouts, attend_heads(): lax.map(lambda trio: attend(trio[0], trio[1], trio[2]), (query_rows, key_...  9.85 us
    reshape x5, local copies, waits for them, and re-layouts, head_major(): return flat.reshape(flat.shape[0], -1, HEAD_DIM).transpose(1, 0, 2)  9.48 us
    reduce_sum x24, other arithmetic, attend(): total_length = jnp.sum(weights, axis=1, keepdims=True)  8.38 us
    reduce_sum x2, other arithmetic, select_rows(): jnp.sum(jnp.where(picks[:, None, :, None], grouped, jnp.zeros((), split.d...  7.08 us
  transfers between devices with their start and end apart: 7, of which 1 were waited for; matrix products, arithmetic and copies ran while one was open for 40% of the time, Pallas kernels for 0%

commit v1 on v0

v1 whole, which is shorter than its diff:
```python
import functools
import math

import jax
import jax.numpy as jnp
import numpy as np
from jax import lax
from jax.experimental import pallas as pl
from jax.experimental.pallas import tpu as pltpu
from jax.sharding import PartitionSpec as P

D = 768
HEAD_DIM = 48
GRID_W = 256
LANES = 128
MESH = pl.DeviceIdType.MESH
F32 = jnp.float32
BF16 = jnp.bfloat16


def angle_tables(positions):
    quarter = D // 4
    freq = np.exp(
        -np.log(np.float32(10000.0)) * np.arange(quarter, dtype=np.float32) / np.float32(quarter)
    ).astype(np.float32)
    angle = np.asarray(positions, np.float32)[..., None] * freq
    return np.concatenate([np.sin(angle), np.cos(angle)], axis=-1).astype(np.float32)


def windows(heads):
    spans = []
    for head in range(heads):
        low = head * HEAD_DIM // LANES
        high = (head * HEAD_DIM + HEAD_DIM - 1) // LANES
        spans.append((low, high + 1))
    return spans


def lane_mask(head, low, high):
    lane = lax.broadcasted_iota(jnp.int32, (1, (high - low) * LANES), 1) + low * LANES
    return (lane >= head * HEAD_DIM) & (lane < (head + 1) * HEAD_DIM)


def attend_tile(query, load_keys, load_values, heads, width):
    rows = query.shape[0]
    tiles = width // LANES
    acc = [None] * tiles
    top = [None] * tiles
    tot = [None] * tiles
    factor = HEAD_DIM**-0.5 * math.log2(math.e)

    def put(store, tile, mask, part):
        part = jnp.broadcast_to(part, (rows, LANES))
        store[tile] = part if store[tile] is None else jnp.where(mask, part, store[tile])

    for head, (low, high) in enumerate(windows(heads)):
        mask = lane_mask(head, low, high)
        q = query[:, low * LANES : high * LANES]
        q = jnp.where(mask, q, jnp.zeros((), q.dtype))
        scores = lax.dot_general(
            q, load_keys(low, high), (((1,), (1,)), ((), ())), preferred_element_type=F32
        )
        best = jnp.max(scores, axis=1, keepdims=True)
        e = jnp.exp2((scores - best) * factor)
        total = jnp.sum(e, axis=1, keepdims=True)
        out = jnp.dot(e.astype(BF16), load_values(low, high), preferred_element_type=F32)
        for tile in range(low, high):
            at = slice((tile - low) * LANES, (tile - low + 1) * LANES)
            put(acc, tile, mask[:, at], out[:, at])
            put(top, tile, mask[:, at], best)
            put(tot, tile, mask[:, at], total)
    return tuple(jnp.concatenate(x, axis=1) for x in (acc, top, tot))


def kernel(
    n, rate_two, rate_three, heads,
    tokens_ref, index_ref, offset_ref, gain_ref, wq_ref, wk_ref, wv_ref, wo_ref, row_ref, col_ref,
    out_ref,
    hidden, query, query_two, query_three, kv, kv_in, kv_two, kv_three,
    acc_own, top_own, tot_own, acc_far, top_far, tot_far,
    acc_two, top_two, tot_two, acc_three, top_three, tot_three,
    attn, attn_in, wo_send, wo_in,
    sem_dense, sem_two, sem_three, sem_attn, sem_wo,
):
    rows = tokens_ref.shape[0]
    width = wq_ref.shape[1]
    me = lax.axis_index("seq")
    core = lax.axis_index("head")
    rows_two = rows // rate_two
    rows_three = rows // rate_three
    group = 2 * rate_two
    pairs = n // 2
    sub_pairs = group // 2
    side = lax.rem(me, 2)
    pair = me // 2
    base = (pair // sub_pairs) * sub_pairs
    inner = pair - base

    barrier = pltpu.get_barrier_semaphore()
    for step in range(1, n):
        pl.semaphore_signal(
            barrier, inc=1, device_id={"seq": lax.rem(me + step, n)}, device_id_type=MESH
        )
    pl.semaphore_signal(barrier, inc=1, device_id={"head": 1 - core}, device_id_type=MESH)

    def remote(src, dst, sems, slot, device):
        return pltpu.make_async_remote_copy(
            src_ref=src, dst_ref=dst, send_sem=sems.at[0, slot], recv_sem=sems.at[1, slot],
            device_id=device, device_id_type=MESH,
        )

    lane = lax.broadcasted_iota(jnp.int32, (1, rows), 1)
    line = lax.broadcasted_iota(jnp.int32, (rows, 1), 0)
    odd = jnp.sum(
        jnp.where(line == lane, (index_ref[...] & 1).astype(F32), 0.0), axis=1, keepdims=True
    )
    per = GRID_W // 2
    row_table = row_ref[me]
    half = D // 2
    for block in range(rows // per):
        at = slice(block * per, (block + 1) * per)
        hidden[at, :half] = tokens_ref[at, :half].astype(F32) + row_table[block : block + 1, :]
        hidden[at, half:] = tokens_ref[at, half:].astype(F32) + jnp.where(
            odd[at] > 0.5, col_ref[1], col_ref[0]
        )
    h = hidden[...]
    mean = jnp.mean(h, axis=1, keepdims=True)
    centred = h - mean
    spread = jnp.mean(centred * centred, axis=1, keepdims=True)
    normed = (centred * lax.rsqrt(spread + 1e-05) * gain_ref[...]).astype(BF16)

    def source_of(i):
        c = i // rows_two
        rest = i - c * rows_two
        b = rest // rows_three
        a = rest - b * rows_three
        return a * rate_three + b * rate_two + c

    order = jnp.where(source_of(line) == lane, 1.0, 0.0).astype(BF16)
    normed = jnp.dot(order, normed, preferred_element_type=F32).astype(BF16)
    kv[:, :width] = jnp.dot(normed, wk_ref[...], preferred_element_type=F32).astype(BF16)
    kv[:, width:] = jnp.dot(normed, wv_ref[...], preferred_element_type=F32).astype(BF16)

    head_of = lax.broadcasted_iota(jnp.int32, (1, width), 1) // HEAD_DIM
    off_two = jnp.zeros((1, width), jnp.int32)
    off_three = jnp.zeros((1, width), jnp.int32)
    for head in range(heads):
        off_two = jnp.where(head_of == head, offset_ref[0, head], off_two)
        off_three = jnp.where(head_of == head, offset_ref[1, head], off_three)

    def class_mask(offset, index, rate):
        residue = index if rate == rate_two else (
            index // (rate_three // rate_two) + rate_two * (index % (rate_three // rate_two))
        )
        return offset == residue

    def select(ref, at, offset, rate):
        count = rows // rate
        out = ref[0:count, at]
        for index in range(1, rate):
            out = jnp.where(
                class_mask(offset, index, rate), ref[index * count : (index + 1) * count, at], out
            )
        return out

    keys_at, values_at = slice(0, width), slice(width, 2 * width)

    def select_kv(ref, buffer, slot, offset, rate):
        buffer[slot, :, keys_at] = select(ref, keys_at, offset, rate)
        buffer[slot, :, values_at] = select(ref, values_at, offset, rate)

    wo_send[...] = wo_ref[:, pl.ds(pl.multiple_of((1 - core) * width, width), width)]
    select_kv(kv, kv_two, 0, off_two, rate_two)
    select_kv(kv, kv_three, 0, off_three, rate_three)

    pl.semaphore_wait(barrier, n)
    copies = []

    def begin(copy):
        copy.start()
        copies.append(copy)
        return copy

    dense = begin(remote(kv, kv_in, sem_dense, 0, {"seq": me + 1 - 2 * side}))
    two, three = [], []
    for step in range(1, sub_pairs):
        for flip in range(2):
            slot = 2 * step + flip
            target = 2 * (base + lax.rem(inner + step, sub_pairs)) + lax.rem(side + flip, 2)
            two.append(
                begin(remote(kv_two.at[0], kv_two.at[slot], sem_two, slot, {"seq": target}))
            )
    for step in range(1, pairs):
        for flip in range(2):
            slot = 2 * step + flip
            target = 2 * lax.rem(pair + step, pairs) + lax.rem(side + flip, 2)
            three.append(
                begin(remote(kv_three.at[0], kv_three.at[slot], sem_three, slot, {"seq": target}))
            )
    wo_copy = begin(remote(wo_send, wo_in, sem_wo, 0, {"head": 1 - core}))

    query[...] = jnp.dot(normed, wq_ref[...], preferred_element_type=F32).astype(BF16)
    query_two[...] = select(query, keys_at, off_two, rate_two)
    query_three[...] = select(query, keys_at, off_three, rate_three)

    def flat_loader(ref, start):
        return lambda low, high: ref[:, start + low * LANES : start + high * LANES]

    def slot_loader(ref, start):
        def load(low, high):
            x = ref[:, :, start + low * LANES : start + high * LANES]
            slots, count, span = x.shape
            if count % 16:
                x = x.astype(F32)
            return x.reshape(slots * count, span).astype(BF16)

        return load

    def run(q_ref, keys, values, acc, top, tot):
        total = q_ref.shape[0]
        tile = min(128, total)

        def step(i, carry):
            at = pl.ds(pl.multiple_of(i * tile, tile), tile)
            a, m, t = attend_tile(q_ref[at, :], keys, values, heads, width)
            acc[at, :] = a
            top[at, :] = m
            tot[at, :] = t
            return carry

        if total == tile:
            a, m, t = attend_tile(q_ref[...], keys, values, heads, width)
            acc[...] = a
            top[...] = m
            tot[...] = t
        else:
            lax.fori_loop(0, total // tile, step, 0)

    run(query, flat_loader(kv, 0), flat_loader(kv, width), acc_own, top_own, tot_own)
    dense.wait_recv()
    select_kv(kv_in, kv_two, 1, off_two, rate_two)
    select_kv(kv_in, kv_three, 1, off_three, rate_three)
    run(query, flat_loader(kv_in, 0), flat_loader(kv_in, width), acc_far, top_far, tot_far)
    for copy in two:
        copy.wait_recv()
    run(query_two, slot_loader(kv_two, 0), slot_loader(kv_two, width), acc_two, top_two, tot_two)
    for copy in three:
        copy.wait_recv()
    run(
        query_three, slot_loader(kv_three, 0), slot_loader(kv_three, width),
        acc_three, top_three, tot_three,
    )

    factor = HEAD_DIM**-0.5 * math.log2(math.e)
    ratio = rate_three // rate_two
    for block in range(rate_three):
        at = slice(block * rows_three, (block + 1) * rows_three)
        inner_at = slice((block % ratio) * rows_three, (block % ratio + 1) * rows_three)
        takes_two = class_mask(off_two, block // ratio, rate_two)
        takes_three = class_mask(off_three, block, rate_three)
        m_own, m_far = top_own[at, :], top_far[at, :]
        best = jnp.maximum(m_own, m_far)
        m_two = jnp.where(takes_two, top_two[inner_at, :], m_own)
        m_three = jnp.where(takes_three, top_three[...], m_own)
        best = jnp.maximum(jnp.maximum(best, m_two), m_three)
        u_own = jnp.exp2((m_own - best) * factor)
        u_far = jnp.exp2((m_far - best) * factor)
        u_two = jnp.where(takes_two, jnp.exp2((m_two - best) * factor), 0.0)
        u_three = jnp.where(takes_three, jnp.exp2((m_three - best) * factor), 0.0)
        summed = (
            u_own * acc_own[at, :] + u_far * acc_far[at, :]
            + u_two * acc_two[inner_at, :] + u_three * acc_three[...]
        )
        total = (
            u_own * tot_own[at, :] + u_far * tot_far[at, :]
            + u_two * tot_two[inner_at, :] + u_three * tot_three[...]
        )
        hidden_rows = summed / total
        acc_own[at, :] = hidden_rows
    back = jnp.where(source_of(lane) == line, 1.0, 0.0).astype(BF16)
    attn[...] = jnp.dot(back, acc_own[...].astype(BF16), preferred_element_type=F32).astype(BF16)
    attn_copy = begin(remote(attn, attn_in, sem_attn, 0, {"head": 1 - core}))
    mine = pl.ds(pl.multiple_of(core * width, width), width)
    out_ref[...] = hidden[:, mine] + jnp.dot(
        attn[...], wo_ref[:, mine], preferred_element_type=F32
    )
    wo_copy.wait_recv()
    attn_copy.wait_recv()
    out_ref[...] += jnp.dot(attn_in[...], wo_in[...], preferred_element_type=F32)
    for copy in copies:
        copy.wait_send()


def body(n, tokens, tile_index, dilation_offset, norm_gain, w_query, w_key, w_value, w_out):
    rows = tokens.shape[0]
    width = w_query.shape[1]
    heads = width // HEAD_DIM
    rate_two = min(16, n // 4)
    rate_three = n // 2
    per = GRID_W // 2
    grid_rows = rows // per
    row_table = jnp.asarray(
        angle_tables(np.arange(n * grid_rows).reshape(n, grid_rows)), F32
    )
    col_table = jnp.asarray(angle_tables(np.arange(GRID_W).reshape(per, 2).T), F32)
    rows_two, rows_three = rows // rate_two, rows // rate_three
    group = 2 * rate_two
    vmem = pl.BlockSpec(memory_space=pltpu.VMEM)

    def trio(count):
        return [pltpu.VMEM((count, width), F32)] * 3

    return pl.pallas_call(
        functools.partial(kernel, n, rate_two, rate_three, heads),
        out_shape=jax.ShapeDtypeStruct((rows, width), F32),
        in_specs=[
            vmem, vmem, pl.BlockSpec(memory_space=pltpu.SMEM), vmem, vmem, vmem, vmem, vmem,
            vmem, vmem,
        ],
        out_specs=vmem,
        scratch_shapes=[
            pltpu.VMEM((rows, D), F32),
            pltpu.VMEM((rows, width), BF16),
            pltpu.VMEM((rows_two, width), BF16),
            pltpu.VMEM((rows_three, width), BF16),
            pltpu.VMEM((rows, 2 * width), BF16),
            pltpu.VMEM((rows, 2 * width), BF16),
            pltpu.VMEM((group, rows_two, 2 * width), BF16),
            pltpu.VMEM((n, rows_three, 2 * width), BF16),
            *trio(rows), *trio(rows), *trio(rows_two), *trio(rows_three),
            pltpu.VMEM((rows, width), BF16),
            pltpu.VMEM((rows, width), BF16),
            pltpu.VMEM((width, width), BF16),
            pltpu.VMEM((width, width), BF16),
            pltpu.SemaphoreType.DMA((2, 1)),
            pltpu.SemaphoreType.DMA((2, group)),
            pltpu.SemaphoreType.DMA((2, n)),
            pltpu.SemaphoreType.DMA((2, 1)),
            pltpu.SemaphoreType.DMA((2, 1)),
        ],
        compiler_params=pltpu.CompilerParams(
            collective_id=0, has_side_effects=True, vmem_limit_bytes=48 * 1024 * 1024
        ),
    )(
        tokens, tile_index.reshape(1, rows), dilation_offset, norm_gain.reshape(1, D),
        w_query, w_key, w_value, w_out, row_table, col_table,
    )


def solution(mesh):
    placed = (
        P(("slide", "seq"), None),
        P(("slide", "seq")),
        P(None, "head"),
        P(),
        P(None, "head"),
        P(None, "head"),
        P(None, "head"),
        P("head", None),
    )
    return jax.shard_map(
        functools.partial(body, mesh.shape["seq"]), mesh=mesh, in_specs=placed,
        out_specs=P(("slide", "seq"), "head"), check_vma=False,
    )
```

time: 235 us -> 71.7 us (0.31)
  the two profiles are of different devices: /device:TPU:0 before, /device:TPU:9 now
where the time goes in v1:
time: 71.7 us; the launch traced here: 71.2 us
  Pallas kernels  62.4 us (87%)
  local copies, waits for them, and re-layouts  8.78 us (12%)
    pallas_call x1, Pallas kernels, body(): pl.pallas_call(functools.partial(kernel, n, rate_two, rate_three, heads),...  62.4 us
    unnamed x19, local copies, waits for them, and re-layouts  8.07 us

profile of v1, /device:TPU:9, one launch (start us, length us, event | category | flops | bytes accessed | tf_op | source)
XLA Modules:
  0.0 71.2 jit_solution(1903153421438647730)
XLA Ops:
  0.0 0.0 copy-start.7
  0.0 0.0 copy-start.8
  0.0 0.7 %reshape.7.gain_ref = f32[1,768]{1,0:T(1,128)S(1)} reshape(f32[768]{0:T(1024)} %param.13) | data formatting | bytes 6144 | tf_op jit(solution)/shard_map/reshape | solution.py:345
  0.7 0.0 copy-done.7
  0.7 0.0 copy-done.8
  0.7 0.0 copy-start
  0.7 1.1 %copy-done = bf16[512,768]{1,0:T(8,128)(2,1)S(1)} copy-done((bf16[512,768]{1,0:T(8,128)(2,1)S(1)}, bf16[512,768]{1,0:T(8,128)(2,1)}, u32[]{:S(2)}) %copy-start) | copy-done | bytes 786456
  1.9 0.0 copy-start.1
  1.9 1.1 %copy-done.1 = bf16[768,384]{1,0:T(8,128)(2,1)S(1)} copy-done((bf16[768,384]{1,0:T(8,128)(2,1)S(1)}, bf16[768,384]{1,0:T(8,128)(2,1)}, u32[]{:S(2)}) %copy-start.1) | copy-done | bytes 589848
  2.9 0.0 copy-start.2
  2.9 1.1 %copy-done.2 = bf16[768,384]{1,0:T(8,128)(2,1)S(1)} copy-done((bf16[768,384]{1,0:T(8,128)(2,1)S(1)}, bf16[768,384]{1,0:T(8,128)(2,1)}, u32[]{:S(2)}) %copy-start.2) | copy-done | bytes 589848
  4.0 0.0 copy-start.3
  4.0 1.1 %copy-done.3 = bf16[768,384]{1,0:T(8,128)(2,1)S(1)} copy-done((bf16[768,384]{1,0:T(8,128)(2,1)S(1)}, bf16[768,384]{1,0:T(8,128)(2,1)}, u32[]{:S(2)}) %copy-start.3) | copy-done | bytes 589848
  5.1 0.0 copy-start.4
  5.1 1.1 %copy-done.4 = bf16[384,768]{1,0:T(8,128)(2,1)S(1)} copy-done((bf16[384,768]{1,0:T(8,128)(2,1)S(1)}, bf16[384,768]{1,0:T(8,128)(2,1)}, u32[]{:S(2)}) %copy-start.4) | copy-done | bytes 589848
  6.1 0.0 copy-start.5
  6.1 1.0 %copy-done.5 = f32[2,128,384]{2,1,0:T(8,128)S(1)} copy-done((f32[2,128,384]{2,1,0:T(8,128)S(1)}, f32[2,128,384]{2,1,0:T(8,128)}, u32[]{:S(2)}) %copy-start.5) | copy-done | bytes 393240
  7.1 0.0 copy-start.6
  7.1 0.8 %copy-done.6 = f32[8,4,384]{2,1,0:T(4,128)S(1)} copy-done((f32[8,4,384]{2,1,0:T(4,128)S(1)}, f32[8,4,384]{2,1,0:T(4,128)}, u32[]{:S(2)}) %copy-start.6) | copy-done | bytes 49176
  7.9 62.4 %shard_map.100 = f32[512,384]{1,0:T(8,128)S(1)} custom-call(bf16[512,768]{1,0:T(8,128)(2,1)S(1)} %copy-done, s32[1,512]{1,0:T(1,128)S(1)} %bitcast.1, s32[2,8]{1,0:T(2,128)S(1)} %copy-done.8, f32[1,768]{1,0:T(1,128)S(1)} %reshape.7.gain_ref, bf16[768,384]{1,0:T(8,128)(2,1)S(1)} %copy-done.1, bf16[768,384]{1,0:T(8,128)(2,1)S(1)} %copy-done.2, ...), custom_call_target="tpu_custom_call" | custom-call | tf_op jit(solution)/shard_map/pallas_call | solution.py:313
  70.4 0.9 %copy.12 = f32[512,384]{1,0:T(8,128)} copy(f32[512,384]{1,0:T(8,128)S(1)} %shard_map.100) | data formatting | bytes 1572864
Async XLA Ops:
  0.0 0.7 %copy-start.7 = (s32[512]{0:T(512)S(1)}, s32[512]{0:T(512)}, u32[]{:S(2)}) copy-start(s32[512]{0:T(512)} %param.11) | copy-start | bytes 6148
  0.0 0.7 %copy-start.8 = (s32[2,8]{1,0:T(2,128)S(1)}, s32[2,8]{1,0:T(2,128)}, u32[]{:S(2)}) copy-start(s32[2,8]{1,0:T(2,128)} %offset_ref.1) | copy-start | bytes 196
  0.7 1.1 %copy-start = (bf16[512,768]{1,0:T(8,128)(2,1)S(1)}, bf16[512,768]{1,0:T(8,128)(2,1)}, u32[]{:S(2)}) copy-start(bf16[512,768]{1,0:T(8,128)(2,1)} %tokens_ref.1) | copy-start | bytes 2359300
  1.9 1.1 %copy-start.1 = (bf16[768,384]{1,0:T(8,128)(2,1)S(1)}, bf16[768,384]{1,0:T(8,128)(2,1)}, u32[]{:S(2)}) copy-start(bf16[768,384]{1,0:T(8,128)(2,1)} %wq_ref.1) | copy-start | bytes 1769476
  2.9 1.1 %copy-start.2 = (bf16[768,384]{1,0:T(8,128)(2,1)S(1)}, bf16[768,384]{1,0:T(8,128)(2,1)}, u32[]{:S(2)}) copy-start(bf16[768,384]{1,0:T(8,128)(2,1)} %wk_ref.1) | copy-start | bytes 1769476
  4.0 1.1 %copy-start.3 = (bf16[768,384]{1,0:T(8,128)(2,1)S(1)}, bf16[768,384]{1,0:T(8,128)(2,1)}, u32[]{:S(2)}) copy-start(bf16[768,384]{1,0:T(8,128)(2,1)} %wv_ref.1) | copy-start | bytes 1769476
  5.1 1.1 %copy-start.4 = (bf16[384,768]{1,0:T(8,128)(2,1)S(1)}, bf16[384,768]{1,0:T(8,128)(2,1)}, u32[]{:S(2)}) copy-start(bf16[384,768]{1,0:T(8,128)(2,1)} %wo_ref.1) | copy-start | bytes 1769476
  6.1 1.0 %copy-start.5 = (f32[2,128,384]{2,1,0:T(8,128)S(1)}, f32[2,128,384]{2,1,0:T(8,128)}, u32[]{:S(2)}) copy-start(f32[2,128,384]{2,1,0:T(8,128)} %constant.5.clone.col_ref) | copy-start | bytes 1179652
  7.1 0.8 %copy-start.6 = (f32[8,4,384]{2,1,0:T(4,128)S(1)}, f32[8,4,384]{2,1,0:T(4,128)}, u32[]{:S(2)}) copy-start(f32[8,4,384]{2,1,0:T(4,128)} %constant.4.clone.row_ref) | copy-start | bytes 147460

commit v2 on v1

v2 whole, which is shorter than its diff:
```python
import functools
import math

import jax
import jax.numpy as jnp
import numpy as np
from jax import lax
from jax.experimental import pallas as pl
from jax.experimental.pallas import tpu as pltpu
from jax.sharding import PartitionSpec as P

D = 768
HEAD_DIM = 48
GRID_W = 256
LANES = 128
MESH = pl.DeviceIdType.MESH
F32 = jnp.float32
BF16 = jnp.bfloat16


def angle_tables(positions):
    quarter = D // 4
    freq = np.exp(
        -np.log(np.float32(10000.0)) * np.arange(quarter, dtype=np.float32) / np.float32(quarter)
    ).astype(np.float32)
    angle = np.asarray(positions, np.float32)[..., None] * freq
    return np.concatenate([np.sin(angle), np.cos(angle)], axis=-1).astype(np.float32)


def windows(heads):
    spans = []
    for head in range(heads):
        low = head * HEAD_DIM // LANES
        high = (head * HEAD_DIM + HEAD_DIM - 1) // LANES
        spans.append((low, high + 1))
    return spans


def lane_mask(head, low, high):
    lane = lax.broadcasted_iota(jnp.int32, (1, (high - low) * LANES), 1) + low * LANES
    return (lane >= head * HEAD_DIM) & (lane < (head + 1) * HEAD_DIM)


def attend_tile(query, load_keys, load_values, heads, width, packed):
    rows = query.shape[0]
    tiles = width // LANES
    acc = [None] * tiles
    top = [None] * tiles
    tot = [None] * tiles
    stat = jnp.zeros((rows, LANES), F32)
    stat_lane = lax.broadcasted_iota(jnp.int32, (1, LANES), 1)
    factor = HEAD_DIM**-0.5 * math.log2(math.e)

    def put(store, tile, mask, part):
        part = jnp.broadcast_to(part, (rows, LANES))
        store[tile] = part if store[tile] is None else jnp.where(mask, part, store[tile])

    for head, (low, high) in enumerate(windows(heads)):
        mask = lane_mask(head, low, high)
        q = query[:, low * LANES : high * LANES]
        q = jnp.where(mask, q, jnp.zeros((), q.dtype))
        scores = lax.dot_general(
            q, load_keys(low, high), (((1,), (1,)), ((), ())), preferred_element_type=F32
        )
        best = jnp.max(scores, axis=1, keepdims=True)
        e = jnp.exp2((scores - best) * factor)
        total = jnp.sum(e, axis=1, keepdims=True)
        out = jnp.dot(e.astype(BF16), load_values(low, high), preferred_element_type=F32)
        for tile in range(low, high):
            at = slice((tile - low) * LANES, (tile - low + 1) * LANES)
            put(acc, tile, mask[:, at], out[:, at])
            put(top, tile, mask[:, at], best)
            put(tot, tile, mask[:, at], total)
        if packed:
            stat = jnp.where(stat_lane == head, best, stat)
            stat = jnp.where(stat_lane == LANES // 2 + head, total, stat)
    return tuple(jnp.concatenate(x, axis=1) for x in (acc, top, tot)) + (stat,)


def kernel(
    n, rate_two, rate_three, heads,
    tokens_hbm, index_ref, offset_ref, gain_ref, wq_hbm, wk_hbm, wv_hbm, wo_hbm, row_hbm, col_hbm,
    out_ref,
    tokens_ref, wq_ref, wk_ref, wv_ref, wo_ref, row_ref, col_ref,
    hidden, nrm, nrm_in, query, query_far, query_two, query_three, kv, kv_in, kv_two, kv_three,
    acc_own, top_own, tot_own, acc_far, top_far, tot_far,
    acc_two, top_two, tot_two, acc_three, top_three, tot_three,
    stat_two, stat_three, ret_two, ret_three,
    back_two, back_three, back_stat_two, back_stat_three,
    attn, attn_in, wo_send, wo_in,
    sem_load, sem_dense, sem_two, sem_three, sem_pair,
):
    rows = tokens_ref.shape[0]
    width = wq_ref.shape[1]
    me = lax.axis_index("seq")
    core = lax.axis_index("head")
    rows_two = rows // rate_two
    rows_three = rows // rate_three
    pairs = n // 2
    sub_pairs = rate_two
    side = lax.rem(me, 2)
    pair = me // 2
    base = (pair // sub_pairs) * sub_pairs
    inner = pair - base
    partner = {"seq": me + 1 - 2 * side}
    sibling = {"head": 1 - core}

    loads = []
    for slot, (src, dst) in enumerate((
        (tokens_hbm, tokens_ref), (row_hbm.at[me], row_ref), (col_hbm, col_ref),
        (wk_hbm, wk_ref), (wv_hbm, wv_ref), (wq_hbm, wq_ref), (wo_hbm, wo_ref),
    )):
        load = pltpu.make_async_copy(src, dst, sem_load.at[slot])
        load.start()
        loads.append(load)

    barrier = pltpu.get_barrier_semaphore()
    for step in range(1, pairs):
        pl.semaphore_signal(
            barrier, inc=1, device_id={"seq": 2 * lax.rem(pair + step, pairs) + side},
            device_id_type=MESH,
        )
    pl.semaphore_signal(barrier, inc=1, device_id=partner, device_id_type=MESH)
    pl.semaphore_signal(barrier, inc=1, device_id=sibling, device_id_type=MESH)

    def remote(src, dst, sems, slot, device):
        return pltpu.make_async_remote_copy(
            src_ref=src, dst_ref=dst, send_sem=sems.at[0, slot], recv_sem=sems.at[1, slot],
            device_id=device, device_id_type=MESH,
        )

    copies = []

    def begin(copy):
        copy.start()
        copies.append(copy)
        return copy

    lane = lax.broadcasted_iota(jnp.int32, (1, rows), 1)
    line = lax.broadcasted_iota(jnp.int32, (rows, 1), 0)

    def source_of(i):
        c = i // rows_two
        rest = i - c * rows_two
        b = rest // rows_three
        a = rest - b * rows_three
        return a * rate_three + b * rate_two + c

    order = jnp.where(source_of(line) == lane, 1.0, 0.0).astype(BF16)

    odd = jnp.sum(
        jnp.where(line == lane, (index_ref[...].reshape(1, rows) & 1).astype(F32), 0.0),
        axis=1, keepdims=True,
    )
    per = GRID_W // 2
    half = D // 2
    for load in loads[:3]:
        load.wait()
    for block in range(rows // per):
        at = slice(block * per, (block + 1) * per)
        hidden[at, :half] = tokens_ref[at, :half].astype(F32) + row_ref[block : block + 1, :]
        hidden[at, half:] = tokens_ref[at, half:].astype(F32) + jnp.where(
            odd[at] > 0.5, col_ref[1], col_ref[0]
        )
    h = hidden[...]
    mean = jnp.mean(h, axis=1, keepdims=True)
    centred = h - mean
    spread = jnp.mean(centred * centred, axis=1, keepdims=True)
    normed = (
        centred * lax.rsqrt(spread + 1e-05) * gain_ref[...].reshape(1, D)
    ).astype(BF16)
    nrm[...] = jnp.dot(order, normed, preferred_element_type=F32).astype(BF16)

    part = pl.ds(pl.multiple_of(core * (rows // 2), rows // 2), rows // 2)
    pl.semaphore_wait(barrier, pairs + 1)
    dense = begin(remote(nrm.at[part], nrm_in.at[part], sem_dense, 0, partner))
    share = remote(nrm_in.at[part], nrm_in.at[part], sem_dense, 1, sibling)

    def project(source, w_ref):
        return jnp.dot(source[...], w_ref[...], preferred_element_type=F32).astype(BF16)

    for load in loads[3:]:
        load.wait()
    kv[:, :width] = project(nrm, wk_ref)
    kv[:, width:] = project(nrm, wv_ref)

    head_of = lax.broadcasted_iota(jnp.int32, (1, width), 1) // HEAD_DIM
    off_two = jnp.zeros((1, width), jnp.int32)
    off_three = jnp.zeros((1, width), jnp.int32)
    for head in range(heads):
        off_two = jnp.where(head_of == head, offset_ref[0, head], off_two)
        off_three = jnp.where(head_of == head, offset_ref[1, head], off_three)

    def class_mask(offset, index, rate):
        residue = index if rate == rate_two else (
            index // (rate_three // rate_two) + rate_two * (index % (rate_three // rate_two))
        )
        return offset == residue

    def select(ref, at, offset, rate):
        count = rows // rate
        out = ref[0:count, at]
        for index in range(1, rate):
            out = jnp.where(
                class_mask(offset, index, rate), ref[index * count : (index + 1) * count, at], out
            )
        return out

    keys_at, values_at = slice(0, width), slice(width, 2 * width)

    def select_kv(ref, buffer, slot, offset, rate):
        buffer[slot, :, keys_at] = select(ref, keys_at, offset, rate)
        buffer[slot, :, values_at] = select(ref, values_at, offset, rate)

    select_kv(kv, kv_two, 0, off_two, rate_two)
    two, three = [], []
    for step in range(1, sub_pairs):
        target = 2 * (base + lax.rem(inner + step, sub_pairs)) + side
        two.append(begin(remote(kv_two.at[0], kv_two.at[step], sem_two, step, {"seq": target})))
    select_kv(kv, kv_three, 0, off_three, rate_three)
    for step in range(1, pairs):
        target = 2 * lax.rem(pair + step, pairs) + side
        three.append(
            begin(remote(kv_three.at[0], kv_three.at[step], sem_three, step, {"seq": target}))
        )
    wo_send[...] = wo_ref[:, pl.ds(pl.multiple_of((1 - core) * width, width), width)]
    wo_copy = begin(remote(wo_send, wo_in, sem_pair, 0, sibling))

    query[...] = project(nrm, wq_ref)
    query_two[0] = select(query, keys_at, off_two, rate_two)
    query_three[0] = select(query, keys_at, off_three, rate_three)

    def flat_loader(ref, start):
        return lambda low, high: ref[:, start + low * LANES : start + high * LANES]

    def slot_loader(ref, start):
        def load(low, high):
            x = ref[:, :, start + low * LANES : start + high * LANES]
            slots, count, span = x.shape
            if count % 16:
                x = x.astype(F32)
            return x.reshape(slots * count, span).astype(BF16)

        return load

    def run(read, total, tile, keys, values, store, packed=False):
        def step(i, carry):
            store(i, *attend_tile(read(i), keys, values, heads, width, packed))
            return carry

        lax.fori_loop(0, total // tile, step, 0)

    def run_dense(keys_ref, acc, top, tot):
        tile = min(128, rows)

        def at(i):
            return pl.ds(pl.multiple_of(i * tile, tile), tile)

        def store(i, a, m, t, stat):
            acc[at(i), :] = a
            top[at(i), :] = m
            tot[at(i), :] = t

        run(
            lambda i: query[at(i), :], rows, tile, flat_loader(keys_ref, 0),
            flat_loader(keys_ref, width), store,
        )

    def run_slots(q_ref, keys_ref, acc, top, tot, stat):
        count = q_ref.shape[1]
        tile = min(128, count)
        each = count // tile

        def at(i):
            return pl.ds(pl.multiple_of(lax.rem(i, each) * tile, tile), tile)

        def store(i, a, m, t, s):
            acc[i // each, at(i), :] = a
            top[i // each, at(i), :] = m
            tot[i // each, at(i), :] = t
            stat[i // each, at(i), :] = s

        run(
            lambda i: q_ref[i // each, at(i), :], 2 * count, tile, slot_loader(keys_ref, 0),
            slot_loader(keys_ref, width), store, True,
        )

    run_dense(kv, acc_own, top_own, tot_own)
    dense.wait_recv()
    begin(share).wait_recv()
    query_far[...] = project(nrm_in, wq_ref)
    query_two[1] = select(query_far, keys_at, off_two, rate_two)
    query_three[1] = select(query_far, keys_at, off_three, rate_three)
    for copy in two:
        copy.wait_recv()
    run_slots(query_two, kv_two, acc_two, top_two, tot_two, stat_two)
    ret_two[...] = acc_two[1].astype(BF16)
    back = [
        begin(remote(ret_two, back_two, sem_pair, 2, partner)),
        begin(remote(stat_two.at[1], back_stat_two, sem_pair, 3, partner)),
    ]
    kv_in[:, :width] = project(nrm_in, wk_ref)
    kv_in[:, width:] = project(nrm_in, wv_ref)
    for copy in three:
        copy.wait_recv()
    run_slots(query_three, kv_three, acc_three, top_three, tot_three, stat_three)
    ret_three[...] = acc_three[1].astype(BF16)
    back.append(begin(remote(ret_three, back_three, sem_pair, 4, partner)))
    back.append(begin(remote(stat_three.at[1], back_stat_three, sem_pair, 5, partner)))
    run_dense(kv_in, acc_far, top_far, tot_far)
    for copy in back:
        copy.wait_recv()

    def spread(stat, start):
        out = jnp.zeros((stat.shape[0], width), F32)
        for head in range(heads):
            out = jnp.where(head_of == head, stat[:, start + head : start + head + 1], out)
        return out

    factor = HEAD_DIM**-0.5 * math.log2(math.e)

    def merge(terms):
        best = functools.reduce(jnp.maximum, [m for _, m, _ in terms])
        acc = tot = 0.0
        for a, m, t in terms:
            u = jnp.exp2((m - best) * factor)
            acc = acc + u * a
            tot = tot + u * t
        return acc, best, tot

    def join(acc, top, tot, back_acc, back_stat):
        far = back_stat[...]
        a, m, t = merge([
            (acc[0], top[0], tot[0]),
            (back_acc[...].astype(F32), spread(far, 0), spread(far, LANES // 2)),
        ])
        acc[0] = a
        top[0] = m
        tot[0] = t

    join(acc_two, top_two, tot_two, back_two, back_stat_two)
    join(acc_three, top_three, tot_three, back_three, back_stat_three)
    ratio = rate_three // rate_two
    for block in range(rate_three):
        at = slice(block * rows_three, (block + 1) * rows_three)
        inner_at = slice((block % ratio) * rows_three, (block % ratio + 1) * rows_three)
        takes_two = class_mask(off_two, block // ratio, rate_two)
        takes_three = class_mask(off_three, block, rate_three)
        m_own, m_far = top_own[at, :], top_far[at, :]
        m_two, m_three = top_two[0, inner_at, :], top_three[0]
        acc, _, tot = merge([
            (acc_own[at, :], m_own, tot_own[at, :]),
            (acc_far[at, :], m_far, tot_far[at, :]),
            (
                jnp.where(takes_two, acc_two[0, inner_at, :], 0.0),
                jnp.where(takes_two, m_two, m_own),
                jnp.where(takes_two, tot_two[0, inner_at, :], 0.0),
            ),
            (
                jnp.where(takes_three, acc_three[0], 0.0),
                jnp.where(takes_three, m_three, m_own),
                jnp.where(takes_three, tot_three[0], 0.0),
            ),
        ])
        acc_own[at, :] = acc / tot
    undo = jnp.where(source_of(lane) == line, 1.0, 0.0).astype(BF16)
    attn[...] = jnp.dot(undo, acc_own[...].astype(BF16), preferred_element_type=F32).astype(BF16)
    attn_copy = begin(remote(attn, attn_in, sem_pair, 1, sibling))
    mine = pl.ds(pl.multiple_of(core * width, width), width)
    out_ref[...] = hidden[:, mine] + jnp.dot(
        attn[...], wo_ref[:, mine], preferred_element_type=F32
    )
    wo_copy.wait_recv()
    attn_copy.wait_recv()
    out_ref[...] += jnp.dot(attn_in[...], wo_in[...], preferred_element_type=F32)
    for copy in copies:
        copy.wait_send()


def body(n, tokens, tile_index, dilation_offset, norm_gain, w_query, w_key, w_value, w_out):
    rows = tokens.shape[0]
    width = w_query.shape[1]
    heads = width // HEAD_DIM
    rate_two = min(16, n // 4)
    rate_three = n // 2
    per = GRID_W // 2
    grid_rows = rows // per
    row_table = jnp.asarray(
        angle_tables(np.arange(n * grid_rows).reshape(n, grid_rows)), F32
    )
    col_table = jnp.asarray(angle_tables(np.arange(GRID_W).reshape(per, 2).T), F32)
    rows_two, rows_three = rows // rate_two, rows // rate_three
    vmem = pl.BlockSpec(memory_space=pltpu.VMEM)
    hbm = pl.BlockSpec(memory_space=pltpu.HBM)

    def trio(*shape):
        return [pltpu.VMEM((*shape, width), F32)] * 3

    def narrow(*shape):
        return pltpu.VMEM(shape, BF16)

    return pl.pallas_call(
        functools.partial(kernel, n, rate_two, rate_three, heads),
        out_shape=jax.ShapeDtypeStruct((rows, width), F32),
        in_specs=[
            hbm, vmem, pl.BlockSpec(memory_space=pltpu.SMEM), vmem, hbm, hbm, hbm, hbm, hbm, hbm
        ],
        out_specs=vmem,
        scratch_shapes=[
            narrow(rows, D), narrow(D, width), narrow(D, width), narrow(D, width),
            narrow(width, D), pltpu.VMEM((grid_rows, D // 2), F32),
            pltpu.VMEM((2, per, D // 2), F32),
            pltpu.VMEM((rows, D), F32), narrow(rows, D), narrow(rows, D),
            narrow(rows, width), narrow(rows, width),
            narrow(2, rows_two, width), narrow(2, rows_three, width),
            narrow(rows, 2 * width), narrow(rows, 2 * width),
            narrow(rate_two, rows_two, 2 * width), narrow(n // 2, rows_three, 2 * width),
            *trio(rows), *trio(rows), *trio(2, rows_two), *trio(2, rows_three),
            pltpu.VMEM((2, rows_two, LANES), F32), pltpu.VMEM((2, rows_three, LANES), F32),
            narrow(rows_two, width), narrow(rows_three, width),
            narrow(rows_two, width), narrow(rows_three, width),
            pltpu.VMEM((rows_two, LANES), F32), pltpu.VMEM((rows_three, LANES), F32),
            narrow(rows, width), narrow(rows, width),
            narrow(width, width), narrow(width, width),
            pltpu.SemaphoreType.DMA((7,)),
            pltpu.SemaphoreType.DMA((2, 2)),
            pltpu.SemaphoreType.DMA((2, rate_two)),
            pltpu.SemaphoreType.DMA((2, n // 2)),
            pltpu.SemaphoreType.DMA((2, 6)),
        ],
        compiler_params=pltpu.CompilerParams(
            collective_id=0, has_side_effects=True, vmem_limit_bytes=48 * 1024 * 1024
        ),
    )(
        tokens, tile_index, dilation_offset, norm_gain,
        w_query, w_key, w_value, w_out, row_table, col_table,
    )


def solution(mesh):
    placed = (
        P(("slide", "seq"), None),
        P(("slide", "seq")),
        P(None, "head"),
        P(),
        P(None, "head"),
        P(None, "head"),
        P(None, "head"),
        P("head", None),
    )
    return jax.shard_map(
        functools.partial(body, mesh.shape["seq"]), mesh=mesh, in_specs=placed,
        out_specs=P(("slide", "seq"), "head"), check_vma=False,
    )
```

time: 71.7 us -> 61.6 us (0.86)
  the two profiles are of different devices: /device:TPU:9 before, /device:TPU:0 now
where the time goes in v2:
time: 61.6 us; the launch traced here: 60.8 us
  Pallas kernels  50.6 us (82%)
  local copies, waits for them, and re-layouts  10.1 us (16%)
    pallas_call x1, Pallas kernels, body(): pl.pallas_call(functools.partial(kernel, n, rate_two, rate_three, heads),...  50.6 us
    unnamed x21, local copies, waits for them, and re-layouts  10.1 us

profile of v2, /device:TPU:0, one launch (start us, length us, event | category | flops | bytes accessed | tf_op | source)
XLA Modules:
  0.0 60.8 jit_solution(10302765398807424434)
XLA Ops:
  0.0 0.0 copy-start
  0.0 1.1 %copy-done = bf16[512,768]{1,0:T(8,128)(2,1)S(1)} copy-done((bf16[512,768]{1,0:T(8,128)(2,1)S(1)}, bf16[512,768]{1,0:T(8,128)(2,1)}, u32[]{:S(2)}) %copy-start) | copy-done | bytes 786456
  1.1 0.0 copy-start.1
  1.1 1.1 %copy-done.1 = bf16[768,384]{1,0:T(8,128)(2,1)S(1)} copy-done((bf16[768,384]{1,0:T(8,128)(2,1)S(1)}, bf16[768,384]{1,0:T(8,128)(2,1)}, u32[]{:S(2)}) %copy-start.1) | copy-done | bytes 589848
  2.2 0.0 copy-start.2
  2.2 1.1 %copy-done.2 = bf16[768,384]{1,0:T(8,128)(2,1)S(1)} copy-done((bf16[768,384]{1,0:T(8,128)(2,1)S(1)}, bf16[768,384]{1,0:T(8,128)(2,1)}, u32[]{:S(2)}) %copy-start.2) | copy-done | bytes 589848
  3.3 0.0 copy-start.3
  3.3 1.1 %copy-done.3 = bf16[768,384]{1,0:T(8,128)(2,1)S(1)} copy-done((bf16[768,384]{1,0:T(8,128)(2,1)S(1)}, bf16[768,384]{1,0:T(8,128)(2,1)}, u32[]{:S(2)}) %copy-start.3) | copy-done | bytes 589848
  4.3 0.0 copy-start.4
  4.3 1.1 %copy-done.4 = bf16[384,768]{1,0:T(8,128)(2,1)S(1)} copy-done((bf16[384,768]{1,0:T(8,128)(2,1)S(1)}, bf16[384,768]{1,0:T(8,128)(2,1)}, u32[]{:S(2)}) %copy-start.4) | copy-done | bytes 589848
  5.4 0.0 copy-start.5
  5.4 1.0 %copy-done.5 = f32[2,128,384]{2,1,0:T(8,128)S(1)} copy-done((f32[2,128,384]{2,1,0:T(8,128)S(1)}, f32[2,128,384]{2,1,0:T(8,128)}, u32[]{:S(2)}) %copy-start.5) | copy-done | bytes 393240
  6.4 0.0 copy-start.6
  6.4 0.8 %copy-done.6 = f32[8,4,384]{2,1,0:T(4,128)S(1)} copy-done((f32[8,4,384]{2,1,0:T(4,128)S(1)}, f32[8,4,384]{2,1,0:T(4,128)}, u32[]{:S(2)}) %copy-start.6) | copy-done | bytes 49176
  7.2 0.0 copy-start.7
  7.2 0.7 %copy-done.7 = f32[768]{0:T(1024)S(1)} copy-done((f32[768]{0:T(1024)S(1)}, f32[768]{0:T(1024)}, u32[]{:S(2)}) %copy-start.7) | copy-done | bytes 3096
  7.9 0.0 copy-start.8
  7.9 0.7 %copy-done.8 = s32[512]{0:T(512)S(1)} copy-done((s32[512]{0:T(512)S(1)}, s32[512]{0:T(512)}, u32[]{:S(2)}) %copy-start.8) | copy-done | bytes 2072
  8.6 0.0 copy-start.9
  8.6 0.7 %copy-done.9 = s32[2,8]{1,0:T(2,128)S(1)} copy-done((s32[2,8]{1,0:T(2,128)S(1)}, s32[2,8]{1,0:T(2,128)}, u32[]{:S(2)}) %copy-start.9) | copy-done | bytes 88
  9.2 50.6 %shard_map.100 = f32[512,384]{1,0:T(8,128)S(1)} custom-call(bf16[512,768]{1,0:T(8,128)(2,1)S(1)} %copy-done, s32[512]{0:T(512)S(1)} %copy-done.8, s32[2,8]{1,0:T(2,128)S(1)} %copy-done.9, f32[768]{0:T(1024)S(1)} %copy-done.7, bf16[768,384]{1,0:T(8,128)(2,1)S(1)} %copy-done.1, bf16[768,384]{1,0:T(8,128)(2,1)S(1)} %copy-done.2, ...), custom_call_target="tpu_custom_call" | custom-call | tf_op jit(solution)/shard_map/pallas_call | solution.py:402
  59.9 0.9 %copy.12 = f32[512,384]{1,0:T(8,128)} copy(f32[512,384]{1,0:T(8,128)S(1)} %shard_map.100) | data formatting | bytes 1572864
Async XLA Ops:
  0.0 1.1 %copy-start = (bf16[512,768]{1,0:T(8,128)(2,1)S(1)}, bf16[512,768]{1,0:T(8,128)(2,1)}, u32[]{:S(2)}) copy-start(bf16[512,768]{1,0:T(8,128)(2,1)} %tokens_hbm.1) | copy-start | bytes 2359300
  1.1 1.1 %copy-start.1 = (bf16[768,384]{1,0:T(8,128)(2,1)S(1)}, bf16[768,384]{1,0:T(8,128)(2,1)}, u32[]{:S(2)}) copy-start(bf16[768,384]{1,0:T(8,128)(2,1)} %wq_hbm.1) | copy-start | bytes 1769476
  2.2 1.1 %copy-start.2 = (bf16[768,384]{1,0:T(8,128)(2,1)S(1)}, bf16[768,384]{1,0:T(8,128)(2,1)}, u32[]{:S(2)}) copy-start(bf16[768,384]{1,0:T(8,128)(2,1)} %wk_hbm.1) | copy-start | bytes 1769476
  3.3 1.1 %copy-start.3 = (bf16[768,384]{1,0:T(8,128)(2,1)S(1)}, bf16[768,384]{1,0:T(8,128)(2,1)}, u32[]{:S(2)}) copy-start(bf16[768,384]{1,0:T(8,128)(2,1)} %wv_hbm.1) | copy-start | bytes 1769476
  4.3 1.1 %copy-start.4 = (bf16[384,768]{1,0:T(8,128)(2,1)S(1)}, bf16[384,768]{1,0:T(8,128)(2,1)}, u32[]{:S(2)}) copy-start(bf16[384,768]{1,0:T(8,128)(2,1)} %wo_hbm.1) | copy-start | bytes 1769476
  5.4 1.0 %copy-start.5 = (f32[2,128,384]{2,1,0:T(8,128)S(1)}, f32[2,128,384]{2,1,0:T(8,128)}, u32[]{:S(2)}) copy-start(f32[2,128,384]{2,1,0:T(8,128)} %constant.5.clone.col_hbm) | copy-start | bytes 1179652
  6.4 0.8 %copy-start.6 = (f32[8,4,384]{2,1,0:T(4,128)S(1)}, f32[8,4,384]{2,1,0:T(4,128)}, u32[]{:S(2)}) copy-start(f32[8,4,384]{2,1,0:T(4,128)} %constant.4.clone.row_hbm) | copy-start | bytes 147460
  7.2 0.7 %copy-start.7 = (f32[768]{0:T(1024)S(1)}, f32[768]{0:T(1024)}, u32[]{:S(2)}) copy-start(f32[768]{0:T(1024)} %gain_ref.1) | copy-start | bytes 9220
  7.9 0.7 %copy-start.8 = (s32[512]{0:T(512)S(1)}, s32[512]{0:T(512)}, u32[]{:S(2)}) copy-start(s32[512]{0:T(512)} %index_ref.1) | copy-start | bytes 6148
  8.6 0.7 %copy-start.9 = (s32[2,8]{1,0:T(2,128)S(1)}, s32[2,8]{1,0:T(2,128)}, u32[]{:S(2)}) copy-start(s32[2,8]{1,0:T(2,128)} %offset_ref.1) | copy-start | bytes 196
